TPU v7x, 32 devices: a whole 2x2x4 slice. The times are simulated.
32 devices in a mesh: pipe: 8 (over y, x, core), dp: 4 (over z).
Axes of the slice: x: 2, y: 2, z: 4, core: 2. Of those that a mesh axis runs over, the one named last changes fastest.
Arguments:
- up_input: bfloat16 [4, 256, 1536], P(None, 'dp'), may hold values from -6 to 6
- down_input: bfloat16 [4, 256, 1536], P(None, 'dp'), may hold values from -6 to 6
- up_cotangent: bfloat16 [4, 256, 1536], P(None, 'dp'), may hold values from -6 to 6
- down_cotangent: bfloat16 [4, 256, 1536], P(None, 'dp'), may hold values from -6 to 6
- weights: bfloat16 [8, 1536, 1536], P('pipe'), may hold values from -0.15625 to 0.15625
Outputs:
- section_outputs: bfloat16 [2, 8, 4, 256, 1536], P(None, 'pipe', None, 'dp')
- input_grads: bfloat16 [2, 8, 4, 256, 1536], P(None, 'pipe', None, 'dp')
- weight_grads: float32 [8, 1536, 1536], P('pipe', 'dp')
All inputs are finite; a program needn't handle non-finite values.
Results may differ from a plain program's by a relative error of at most 0.015.
Values may be sent and summed in bfloat16 or wider, within the bound.
A program may use at most 128 MiB of HBM per device.

v0:
```python
import jax
import jax.numpy as jnp
from jax import lax
from jax.sharding import PartitionSpec as P

NORM_EPS = 1e-06


def passed_along(block, axis, distance):
    devices = range(lax.axis_size(axis))
    route = [(i - distance, i) for i in devices if i - distance in devices]
    return lax.ppermute(block, axis, route)


def from_partner(array, axis, apart):
    return lax.ppermute(array, axis, [(i, i ^ 1 << apart) for i in range(lax.axis_size(axis))])


def forward_layer(layer_in, weight):
    inputs_f32 = layer_in.astype(jnp.float32)
    inv_rms = lax.rsqrt(jnp.mean(inputs_f32 * inputs_f32, axis=-1, keepdims=True) + NORM_EPS)
    hidden = (inputs_f32 * inv_rms).astype(jnp.bfloat16)
    pre_act = jnp.dot(hidden, weight, preferred_element_type=jnp.float32)
    layer_out = (inputs_f32 + jax.nn.silu(pre_act)).astype(jnp.bfloat16)
    return (layer_out, hidden, pre_act)


def backward_layer(layer_in, pre_act, weight, grad_out):
    inputs_f32 = layer_in.astype(jnp.float32)
    inv_rms = lax.rsqrt(jnp.mean(inputs_f32 * inputs_f32, axis=-1, keepdims=True) + NORM_EPS)
    grad_f32 = grad_out.astype(jnp.float32)
    sigmoid_pre = jax.nn.sigmoid(pre_act)
    grad_pre = (grad_f32 * sigmoid_pre * (1.0 + pre_act * (1.0 - sigmoid_pre))).astype(jnp.bfloat16)
    grad_hidden = lax.dot_general(
        grad_pre, weight, (((1,), (1,)), ((), ())), preferred_element_type=jnp.float32
    )
    inner = jnp.mean(grad_hidden * inputs_f32, axis=-1, keepdims=True)
    grad_in = grad_f32 + inv_rms * (grad_hidden - inputs_f32 * inv_rms * inv_rms * inner)
    return (grad_in.astype(jnp.bfloat16), grad_pre)


def send_forward(layer_out, upward):
    if upward:
        return passed_along(layer_out, "pipe", 1)
    return passed_along(layer_out, "pipe", -1)


def send_backward(grad_in, upward):
    if upward:
        return passed_along(grad_in, "pipe", -1)
    return passed_along(grad_in, "pipe", 1)


def empty_forward(source):
    zero_bf = jnp.zeros(source.shape, jnp.bfloat16)
    return (
        jnp.zeros(source.shape[1:], jnp.bfloat16),
        zero_bf,
        zero_bf,
        jnp.zeros(source.shape, jnp.float32),
        zero_bf,
    )


def empty_backward(source):
    zero_bf = jnp.zeros(source.shape, jnp.bfloat16)
    return (jnp.zeros(source.shape[1:], jnp.bfloat16), zero_bf, zero_bf)


def forward_step(carry_state, step_id, position, source, weight, upward):
    received, saved_in, saved_out, saved_pre, saved_hidden = carry_state
    micro_total = source.shape[0]
    micro_id = step_id - position
    is_valid = jnp.logical_and(micro_id >= 0, micro_id < micro_total)
    slot_index = jnp.clip(micro_id, 0, micro_total - 1)
    fresh_input = lax.dynamic_index_in_dim(source, slot_index, 0, keepdims=False)
    layer_in = jnp.where(position == 0, fresh_input, received)

    def forward_compute(operand):
        layer_out, hidden, pre_act = forward_layer(operand, weight)
        stored = (
            saved_in.at[slot_index].set(operand),
            saved_out.at[slot_index].set(layer_out),
            saved_pre.at[slot_index].set(pre_act),
            saved_hidden.at[slot_index].set(hidden),
        )
        return (stored, layer_out)

    def forward_skip_work(operand):
        return ((saved_in, saved_out, saved_pre, saved_hidden), jnp.zeros_like(operand))

    stored, layer_out = lax.cond(is_valid, forward_compute, forward_skip_work, layer_in)
    return (send_forward(layer_out, upward),) + stored


def backward_step(carry_state, step_id, position, cotangent, saved, weight, upward):
    received, saved_grad, saved_dpre = carry_state
    saved_in = saved[0]
    saved_pre = saved[2]
    micro_total = cotangent.shape[0]
    micro_id = step_id - position
    is_valid = jnp.logical_and(micro_id >= 0, micro_id < micro_total)
    slot_index = jnp.clip(micro_id, 0, micro_total - 1)
    fresh_grad = lax.dynamic_index_in_dim(cotangent, slot_index, 0, keepdims=False)
    grad_out = jnp.where(position == 0, fresh_grad, received)

    def backward_compute(operand):
        layer_in = lax.dynamic_index_in_dim(saved_in, slot_index, 0, keepdims=False)
        pre_act = lax.dynamic_index_in_dim(saved_pre, slot_index, 0, keepdims=False)
        grad_in, grad_pre = backward_layer(layer_in, pre_act, weight, operand)
        stored = (saved_grad.at[slot_index].set(grad_in), saved_dpre.at[slot_index].set(grad_pre))
        return (stored, grad_in)

    def backward_skip_work(operand):
        return ((saved_grad, saved_dpre), jnp.zeros_like(operand))

    stored, grad_in = lax.cond(is_valid, backward_compute, backward_skip_work, grad_out)
    return (send_backward(grad_in, upward),) + stored


def local(up_input, down_input, up_cotangent, down_cotangent, weights):
    sections = lax.axis_size("pipe")
    replicas = lax.axis_size("dp")
    section_index = lax.axis_index("pipe")
    own_weight = weights[0]
    row_count = own_weight.shape[0] // replicas
    own_rows = lax.dynamic_slice_in_dim(own_weight, lax.axis_index("dp") * row_count, row_count, 0)
    bit_count = sections.bit_length() - 1
    flip_order = list(range(bit_count))
    carried = own_rows
    for bit_id in flip_order:
        carried = from_partner(carried, "pipe", bit_id)
    mirror_weight = lax.all_gather(carried, "dp", axis=0, tiled=True)
    down_position = sections - 1 - section_index
    step_ids = jnp.arange(up_input.shape[0] + sections - 1, dtype=jnp.int32)

    def up_forward(carry_state, step_id):
        return (forward_step(carry_state, step_id, section_index, up_input, own_weight, True), None)

    def down_forward(carry_state, step_id):
        return (
            forward_step(carry_state, step_id, down_position, down_input, mirror_weight, False),
            None,
        )

    up_state, unused = lax.scan(up_forward, empty_forward(up_input), step_ids)
    down_state, unused = lax.scan(down_forward, empty_forward(down_input), step_ids)
    up_saved = up_state[1:]
    down_saved = down_state[1:]

    def up_backward(carry_state, step_id):
        return (
            backward_step(
                carry_state, step_id, down_position, up_cotangent, up_saved, own_weight, True
            ),
            None,
        )

    def down_backward(carry_state, step_id):
        return (
            backward_step(
                carry_state,
                step_id,
                section_index,
                down_cotangent,
                down_saved,
                mirror_weight,
                False,
            ),
            None,
        )

    up_back, unused = lax.scan(up_backward, empty_backward(up_cotangent), step_ids)
    down_back, unused = lax.scan(down_backward, empty_backward(down_cotangent), step_ids)
    model_width = own_weight.shape[1]
    hidden_both = jnp.stack([up_saved[3], down_saved[3]]).reshape(2, -1, model_width)
    dpre_both = jnp.stack([up_back[2], down_back[2]]).reshape(2, -1, model_width)
    grad_term = jnp.einsum(
        "ard,are->dae", hidden_both, dpre_both, preferred_element_type=jnp.float32
    )
    reduced = lax.psum_scatter(
        grad_term.astype(jnp.bfloat16), "dp", scatter_dimension=0, tiled=True
    ).astype(jnp.float32)
    mirror_part = reduced[:, 1, :]
    for bit_id in flip_order:
        mirror_part = from_partner(mirror_part.astype(jnp.bfloat16), "pipe", bit_id).astype(
            mirror_part.dtype
        )
    weight_grads = (reduced[:, 0, :] + mirror_part)[None]
    section_outputs = jnp.stack([up_saved[1], down_saved[1]])[:, None]
    input_grads = jnp.stack([up_back[1], down_back[1]])[:, None]
    return (section_outputs, input_grads, weight_grads)


def solution(mesh):
    return jax.shard_map(
        local,
        mesh=mesh,
        in_specs=(
            P(None, "dp", None),
            P(None, "dp", None),
            P(None, "dp", None),
            P(None, "dp", None),
            P("pipe", None, None),
        ),
        out_specs=(
            P(None, "pipe", None, "dp", None),
            P(None, "pipe", None, "dp", None),
            P("pipe", "dp", None),
        ),
        check_vma=False,
    )
```

profile of v0, /device:TPU:0, one launch (start us, length us, event | category | flops | bytes accessed | tf_op | source)
XLA Modules:
  0.0 1001.1 jit_solution(1658293100250301223)
XLA Ops:
  14.4 26.3 %collective-permute-done.5 = bf16[384,1536]{1,0:T(8,128)(2,1)S(1)} collective-permute-done((bf16[384,1536]{1,0:T(8,128)(2,1)S(1)}, bf16[384,1536]{1,0:T(8,128)(2,1)S(1)}, u32[]{:S(2)}, u32[]{:S(2)}) %collective-permute-start.5) | collective-permute-done | bytes 1179680 | tf_op jit(solution)/shard_map/ppermute | solution.py:16
  42.5 25.7 %collective-permute-done.6 = bf16[384,1536]{1,0:T(8,128)(2,1)S(1)} collective-permute-done((bf16[384,1536]{1,0:T(8,128)(2,1)S(1)}, bf16[384,1536]{1,0:T(8,128)(2,1)S(1)}, u32[]{:S(2)}, u32[]{:S(2)}) %collective-permute-start.6) | collective-permute-done | bytes 1179680 | tf_op jit(solution)/shard_map/ppermute | solution.py:16
  70.6 140.0 %while.80 = (s32[]{:T(128)}, bf16[64,1536]{1,0:T(8,128)(2,1)S(1)}, bf16[4,64,1536]{2,1,0:T(8,128)(2,1)S(1)}, bf16[4,64,1536]{2,1,0:T(8,128)(2,1)}, f32[4,64,1536...) while((s32[]{:T(128)}, bf16[64,1536]{1,0:T(8,128)(2,1)S(1)}, ...), condition=%wide.region_5.6_spmd, body=%wide.region_0.5_spmd.sunk | while | flops 303956064 | bytes 9440422 | solution.py:146
  127.4 14.0 %collective-permute-start = (bf16[64,1536]{1,0:T(8,128)(2,1)S(1)}, bf16[64,1536]{1,0:T(8,128)(2,1)S(1)}, u32[]{:S(2)}, u32[]{:S(2)}) collective-permute-start(bf16[64,1536]{1,0:T(8,128)(2,1)S(1)} %get-tuple-element.1377), channel_id=1, source_target_pairs={{0,4},{4,8},{8,12},{12,16},{16,20},{20,24},{24,28},{1,5},{5,9},{9,... | collective-permute-start | bytes 589832 | tf_op jit(solution)/shard_map/while/body/eval_jaxpr/ppermute | solution.py:12
  152.3 14.0 %collective-permute-start = (bf16[64,1536]{1,0:T(8,128)(2,1)S(1)}, bf16[64,1536]{1,0:T(8,128)(2,1)S(1)}, u32[]{:S(2)}, u32[]{:S(2)}) collective-permute-start(bf16[64,1536]{1,0:T(8,128)(2,1)S(1)} %get-tuple-element.1377), channel_id=1, source_target_pairs={{0,4},{4,8},{8,12},{12,16},{16,20},{20,24},{24,28},{1,5},{5,9},{9,... | collective-permute-start | bytes 589832 | tf_op jit(solution)/shard_map/while/body/eval_jaxpr/ppermute | solution.py:12
  194.6 14.9 %collective-permute-start = (bf16[64,1536]{1,0:T(8,128)(2,1)S(1)}, bf16[64,1536]{1,0:T(8,128)(2,1)S(1)}, u32[]{:S(2)}, u32[]{:S(2)}) collective-permute-start(bf16[64,1536]{1,0:T(8,128)(2,1)S(1)} %get-tuple-element.1377), channel_id=1, source_target_pairs={{0,4},{4,8},{8,12},{12,16},{16,20},{20,24},{24,28},{1,5},{5,9},{9,... | collective-permute-start | bytes 589832 | tf_op jit(solution)/shard_map/while/body/eval_jaxpr/ppermute | solution.py:12
  212.5 203.2 %while.82 = (s32[]{:T(128)}, bf16[64,1536]{1,0:T(8,128)(2,1)S(1)}, bf16[4,64,1536]{2,1,0:T(8,128)(2,1)S(1)}, bf16[4,64,1536]{2,1,0:T(8,128)(2,1)}, s32[11]{0:T(1...) while((s32[]{:T(128)}, bf16[64,1536]{1,0:T(8,128)(2,1)S(1)}, ...), condition=%wide.region_18.19_spmd, body=%wide.region_12.18_spmd.sunk | while | flops 304742496 | bytes 9245062 | solution.py:173
  274.6 69.1 %collective-permute-done.2 = bf16[64,1536]{1,0:T(8,128)(2,1)S(1)} collective-permute-done((bf16[64,1536]{1,0:T(8,128)(2,1)S(1)}, bf16[64,1536]{1,0:T(8,128)(2,1)S(1)}, u32[]{:S(2)}, u32[]{:S(2)}) %collective-permute-start.2) | collective-permute-done | bytes 196640 | tf_op jit(solution)/shard_map/while/body/eval_jaxpr/ppermute | solution.py:12
  345.2 9.8 conditional.10
  383.4 9.8 conditional.10
  419.5 140.5 %while.81 = (s32[]{:T(128)}, bf16[64,1536]{1,0:T(8,128)(2,1)S(1)}, bf16[4,64,1536]{2,1,0:T(8,128)(2,1)S(1)}, bf16[4,64,1536]{2,1,0:T(8,128)(2,1)}, f32[4,64,1536...) while((s32[]{:T(128)}, bf16[64,1536]{1,0:T(8,128)(2,1)S(1)}, ...), condition=%wide.region_11.12_spmd, body=%wide.region_6.11_spmd.sunk | while | flops 303956064 | bytes 9440422 | solution.py:147
  467.9 27.5 %collective-permute-done.1 = bf16[64,1536]{1,0:T(8,128)(2,1)S(1)} collective-permute-done((bf16[64,1536]{1,0:T(8,128)(2,1)S(1)}, bf16[64,1536]{1,0:T(8,128)(2,1)S(1)}, u32[]{:S(2)}, u32[]{:S(2)}) %collective-permute-start.1) | collective-permute-done | bytes 196640 | tf_op jit(solution)/shard_map/while/body/eval_jaxpr/ppermute | solution.py:12
  562.0 156.5 %while.83 = (s32[]{:T(128)}, bf16[64,1536]{1,0:T(8,128)(2,1)S(1)}, bf16[4,64,1536]{2,1,0:T(8,128)(2,1)}, bf16[4,64,1536]{2,1,0:T(8,128)(2,1)}, s32[11]{0:T(128)S...) while((s32[]{:T(128)}, bf16[64,1536]{1,0:T(8,128)(2,1)S(1)}, ...), condition=%wide.region_25.26_spmd, body=%wide.region_19.25_spmd.sunk | while | flops 304742496 | bytes 9246080 | solution.py:174
  563.3 10.3 %conditional.11 = (bf16[4,64,1536]{2,1,0:T(8,128)(2,1)}, bf16[4,64,1536]{2,1,0:T(8,128)(2,1)}, bf16[64,1536]{1,0:T(8,128)(2,1)S(1)}) conditional(s32[]{:T(128)} %convert_element_type.213, (bf16[4,64,1536]{2,1,0:T(8,128)(2,1)}, bf16[4,64,1536]{2,1,0:T(8,128)(2,1)}) %tuple.229, (s32[]{:T(128)}, pred[]{:T(512)}, bf16[4,64,1536]{2,1,0:T(8,128)(2,1)}, ...), branch_computations={%region_20.20_spmd, %region_21.24_spmd} | conditional | flops 304742496 | bytes 8459337 | solution.py:117
  577.2 10.3 %conditional.11 = (bf16[4,64,1536]{2,1,0:T(8,128)(2,1)}, bf16[4,64,1536]{2,1,0:T(8,128)(2,1)}, bf16[64,1536]{1,0:T(8,128)(2,1)S(1)}) conditional(s32[]{:T(128)} %convert_element_type.213, (bf16[4,64,1536]{2,1,0:T(8,128)(2,1)}, bf16[4,64,1536]{2,1,0:T(8,128)(2,1)}) %tuple.229, (s32[]{:T(128)}, pred[]{:T(512)}, bf16[4,64,1536]{2,1,0:T(8,128)(2,1)}, ...), branch_computations={%region_20.20_spmd, %region_21.24_spmd} | conditional | flops 304742496 | bytes 8459337 | solution.py:117
  592.2 10.3 %conditional.11 = (bf16[4,64,1536]{2,1,0:T(8,128)(2,1)}, bf16[4,64,1536]{2,1,0:T(8,128)(2,1)}, bf16[64,1536]{1,0:T(8,128)(2,1)S(1)}) conditional(s32[]{:T(128)} %convert_element_type.213, (bf16[4,64,1536]{2,1,0:T(8,128)(2,1)}, bf16[4,64,1536]{2,1,0:T(8,128)(2,1)}) %tuple.229, (s32[]{:T(128)}, pred[]{:T(512)}, bf16[4,64,1536]{2,1,0:T(8,128)(2,1)}, ...), branch_computations={%region_20.20_spmd, %region_21.24_spmd} | conditional | flops 304742496 | bytes 8459337 | solution.py:117
  608.3 10.3 %conditional.11 = (bf16[4,64,1536]{2,1,0:T(8,128)(2,1)}, bf16[4,64,1536]{2,1,0:T(8,128)(2,1)}, bf16[64,1536]{1,0:T(8,128)(2,1)S(1)}) conditional(s32[]{:T(128)} %convert_element_type.213, (bf16[4,64,1536]{2,1,0:T(8,128)(2,1)}, bf16[4,64,1536]{2,1,0:T(8,128)(2,1)}) %tuple.229, (s32[]{:T(128)}, pred[]{:T(512)}, bf16[4,64,1536]{2,1,0:T(8,128)(2,1)}, ...), branch_computations={%region_20.20_spmd, %region_21.24_spmd} | conditional | flops 304742496 | bytes 8459337 | solution.py:117
  626.9 16.2 %collective-permute-start.3 = (bf16[64,1536]{1,0:T(8,128)(2,1)S(1)}, bf16[64,1536]{1,0:T(8,128)(2,1)S(1)}, u32[]{:S(2)}, u32[]{:S(2)}) collective-permute-start(bf16[64,1536]{1,0:T(8,128)(2,1)S(1)} %get-tuple-element.1423), channel_id=1, source_target_pairs={{0,4},{4,8},{8,12},{12,16},{16,20},{20,24},{24,28},{1,5},{5,9},{9,... | collective-permute-start | bytes 589832 | tf_op jit(solution)/shard_map/while/body/eval_jaxpr/ppermute | solution.py:12
  653.9 16.1 %collective-permute-start.3 = (bf16[64,1536]{1,0:T(8,128)(2,1)S(1)}, bf16[64,1536]{1,0:T(8,128)(2,1)S(1)}, u32[]{:S(2)}, u32[]{:S(2)}) collective-permute-start(bf16[64,1536]{1,0:T(8,128)(2,1)S(1)} %get-tuple-element.1423), channel_id=1, source_target_pairs={{0,4},{4,8},{8,12},{12,16},{16,20},{20,24},{24,28},{1,5},{5,9},{9,... | collective-permute-start | bytes 589832 | tf_op jit(solution)/shard_map/while/body/eval_jaxpr/ppermute | solution.py:12
  700.4 17.0 %collective-permute-start.3 = (bf16[64,1536]{1,0:T(8,128)(2,1)S(1)}, bf16[64,1536]{1,0:T(8,128)(2,1)S(1)}, u32[]{:S(2)}, u32[]{:S(2)}) collective-permute-start(bf16[64,1536]{1,0:T(8,128)(2,1)S(1)} %get-tuple-element.1423), channel_id=1, source_target_pairs={{0,4},{4,8},{8,12},{12,16},{16,20},{20,24},{24,28},{1,5},{5,9},{9,... | collective-permute-start | bytes 589832 | tf_op jit(solution)/shard_map/while/body/eval_jaxpr/ppermute | solution.py:12
  725.4 12.7 %copy.19 = bf16[1536,3072]{1,0:T(8,128)(2,1)} copy(bf16[1536,3072]{0,1:T(8,128)(2,1)} %bitcast.166) | data formatting | bytes 18874368
  738.1 190.1 %reduce-scatter.4.cloned.1.call-done = bf16[384,3072]{1,0:T(8,128)(2,1)} async-done(((bf16[1536,3072]{1,0:T(8,128)(2,1)}), bf16[384,3072]{1,0:T(8,128)(2,1)}) %reduce-scatter.4.cloned.1.call-update) | async-done | bytes 2359312
  935.8 26.5 %collective-permute-done.8 = bf16[384,1536]{0,1:T(8,128)(2,1)S(1)} collective-permute-done((bf16[384,1536]{0,1:T(8,128)(2,1)S(1)}, bf16[384,1536]{0,1:T(8,128)(2,1)S(1)}, u32[]{:S(2)}, u32[]{:S(2)}) %collective-permute-start.8) | collective-permute-done | bytes 1179680 | tf_op jit(solution)/shard_map/ppermute | solution.py:16
  965.7 23.8 %collective-permute-done.9 = bf16[384,1536]{0,1:T(8,128)(2,1)S(1)} collective-permute-done((bf16[384,1536]{0,1:T(8,128)(2,1)S(1)}, bf16[384,1536]{0,1:T(8,128)(2,1)S(1)}, u32[]{:S(2)}, u32[]{:S(2)}) %collective-permute-start.9) | collective-permute-done | bytes 1179680 | tf_op jit(solution)/shard_map/ppermute | solution.py:16
  (330 shorter events, 546.3 us)
Async XLA Ops:
  7.2 411.1 %all-gather.2.cloned.1.call-start = ((), (), s32[]{:S(2)}) async-start(), calls=%async_computation.1 | async-start | bytes 5898240 | tf_op jit(solution)/shard_map/all_gather | solution.py:133
  11.6 29.1 %collective-permute-start.5 = (bf16[384,1536]{1,0:T(8,128)(2,1)S(1)}, bf16[384,1536]{1,0:T(8,128)(2,1)S(1)}, u32[]{:S(2)}, u32[]{:S(2)}) collective-permute-start(bf16[384,1536]{1,0:T(8,128)(2,1)S(1)} %collective-permute-done.4), channel_id=1, source_target_pairs={{0,8},{4,12},{8,0},{12,4},{16,24},{20,28},{24,16},{28,20},{1,9},{5... | collective-permute-start | bytes 3538952 | tf_op jit(solution)/shard_map/ppermute | solution.py:16
  40.7 27.5 %collective-permute-start.6 = (bf16[384,1536]{1,0:T(8,128)(2,1)S(1)}, bf16[384,1536]{1,0:T(8,128)(2,1)S(1)}, u32[]{:S(2)}, u32[]{:S(2)}) collective-permute-start(bf16[384,1536]{1,0:T(8,128)(2,1)S(1)} %collective-permute-done.5), channel_id=1, source_target_pairs={{0,16},{4,20},{8,24},{12,28},{16,0},{20,4},{24,8},{28,12},{1,17},{... | collective-permute-start | bytes 3538952 | tf_op jit(solution)/shard_map/ppermute | solution.py:16
  69.2 858.9 %reduce-scatter.4.cloned.1.call-start = ((), (), s32[]{:S(2)}) async-start(), calls=%async_computation.2 | async-start | bytes 11796480
  127.4 15.1 %collective-permute-start = (bf16[64,1536]{1,0:T(8,128)(2,1)S(1)}, bf16[64,1536]{1,0:T(8,128)(2,1)S(1)}, u32[]{:S(2)}, u32[]{:S(2)}) collective-permute-start(bf16[64,1536]{1,0:T(8,128)(2,1)S(1)} %get-tuple-element.1377), channel_id=1, source_target_pairs={{0,4},{4,8},{8,12},{12,16},{16,20},{20,24},{24,28},{1,5},{5,9},{9,... | collective-permute-start | bytes 589832 | tf_op jit(solution)/shard_map/while/body/eval_jaxpr/ppermute | solution.py:12
  152.3 15.0 %collective-permute-start = (bf16[64,1536]{1,0:T(8,128)(2,1)S(1)}, bf16[64,1536]{1,0:T(8,128)(2,1)S(1)}, u32[]{:S(2)}, u32[]{:S(2)}) collective-permute-start(bf16[64,1536]{1,0:T(8,128)(2,1)S(1)} %get-tuple-element.1377), channel_id=1, source_target_pairs={{0,4},{4,8},{8,12},{12,16},{16,20},{20,24},{24,28},{1,5},{5,9},{9,... | collective-permute-start | bytes 589832 | tf_op jit(solution)/shard_map/while/body/eval_jaxpr/ppermute | solution.py:12
  194.6 15.9 %collective-permute-start = (bf16[64,1536]{1,0:T(8,128)(2,1)S(1)}, bf16[64,1536]{1,0:T(8,128)(2,1)S(1)}, u32[]{:S(2)}, u32[]{:S(2)}) collective-permute-start(bf16[64,1536]{1,0:T(8,128)(2,1)S(1)} %get-tuple-element.1377), channel_id=1, source_target_pairs={{0,4},{4,8},{8,12},{12,16},{16,20},{20,24},{24,28},{1,5},{5,9},{9,... | collective-permute-start | bytes 589832 | tf_op jit(solution)/shard_map/while/body/eval_jaxpr/ppermute | solution.py:12
  223.1 8.6 collective-permute-start.2
  242.3 11.0 %collective-permute-start.2 = (bf16[64,1536]{1,0:T(8,128)(2,1)S(1)}, bf16[64,1536]{1,0:T(8,128)(2,1)S(1)}, u32[]{:S(2)}, u32[]{:S(2)}) collective-permute-start(bf16[64,1536]{1,0:T(8,128)(2,1)S(1)} %get-tuple-element.1409), channel_id=1, source_target_pairs={{4,0},{8,4},{12,8},{16,12},{20,16},{24,20},{28,24},{5,1},{9,5},{13... | collective-permute-start | bytes 589832 | tf_op jit(solution)/shard_map/while/body/eval_jaxpr/ppermute | solution.py:12
  254.7 7.9 collective-permute-start.2
  264.0 7.9 collective-permute-start.2
  273.3 70.4 %collective-permute-start.2 = (bf16[64,1536]{1,0:T(8,128)(2,1)S(1)}, bf16[64,1536]{1,0:T(8,128)(2,1)S(1)}, u32[]{:S(2)}, u32[]{:S(2)}) collective-permute-start(bf16[64,1536]{1,0:T(8,128)(2,1)S(1)} %get-tuple-element.1409), channel_id=1, source_target_pairs={{4,0},{8,4},{12,8},{16,12},{20,16},{24,20},{28,24},{5,1},{9,5},{13... | collective-permute-start | bytes 589832 | tf_op jit(solution)/shard_map/while/body/eval_jaxpr/ppermute | solution.py:12
  355.0 7.9 collective-permute-start.2
  374.1 7.9 collective-permute-start.2
  466.6 28.9 %collective-permute-start.1 = (bf16[64,1536]{1,0:T(8,128)(2,1)S(1)}, bf16[64,1536]{1,0:T(8,128)(2,1)S(1)}, u32[]{:S(2)}, u32[]{:S(2)}) collective-permute-start(bf16[64,1536]{1,0:T(8,128)(2,1)S(1)} %get-tuple-element.1393), channel_id=1, source_target_pairs={{4,0},{8,4},{12,8},{16,12},{20,16},{24,20},{28,24},{5,1},{9,5},{13... | collective-permute-start | bytes 589832 | tf_op jit(solution)/shard_map/while/body/eval_jaxpr/ppermute | solution.py:12
  504.8 7.9 collective-permute-start.1
  522.1 7.9 collective-permute-start.1
  539.4 7.9 collective-permute-start.1
  626.9 17.2 %collective-permute-start.3 = (bf16[64,1536]{1,0:T(8,128)(2,1)S(1)}, bf16[64,1536]{1,0:T(8,128)(2,1)S(1)}, u32[]{:S(2)}, u32[]{:S(2)}) collective-permute-start(bf16[64,1536]{1,0:T(8,128)(2,1)S(1)} %get-tuple-element.1423), channel_id=1, source_target_pairs={{0,4},{4,8},{8,12},{12,16},{16,20},{20,24},{24,28},{1,5},{5,9},{9,... | collective-permute-start | bytes 589832 | tf_op jit(solution)/shard_map/while/body/eval_jaxpr/ppermute | solution.py:12
  653.9 17.2 %collective-permute-start.3 = (bf16[64,1536]{1,0:T(8,128)(2,1)S(1)}, bf16[64,1536]{1,0:T(8,128)(2,1)S(1)}, u32[]{:S(2)}, u32[]{:S(2)}) collective-permute-start(bf16[64,1536]{1,0:T(8,128)(2,1)S(1)} %get-tuple-element.1423), channel_id=1, source_target_pairs={{0,4},{4,8},{8,12},{12,16},{16,20},{20,24},{24,28},{1,5},{5,9},{9,... | collective-permute-start | bytes 589832 | tf_op jit(solution)/shard_map/while/body/eval_jaxpr/ppermute | solution.py:12
  680.9 9.5 collective-permute-start.3
  700.4 18.1 %collective-permute-start.3 = (bf16[64,1536]{1,0:T(8,128)(2,1)S(1)}, bf16[64,1536]{1,0:T(8,128)(2,1)S(1)}, u32[]{:S(2)}, u32[]{:S(2)}) collective-permute-start(bf16[64,1536]{1,0:T(8,128)(2,1)S(1)} %get-tuple-element.1423), channel_id=1, source_target_pairs={{0,4},{4,8},{8,12},{12,16},{16,20},{20,24},{24,28},{1,5},{5,9},{9,... | collective-permute-start | bytes 589832 | tf_op jit(solution)/shard_map/while/body/eval_jaxpr/ppermute | solution.py:12
  934.3 28.0 %collective-permute-start.8 = (bf16[384,1536]{0,1:T(8,128)(2,1)S(1)}, bf16[384,1536]{0,1:T(8,128)(2,1)S(1)}, u32[]{:S(2)}, u32[]{:S(2)}) collective-permute-start(bf16[384,1536]{0,1:T(8,128)(2,1)S(1)} %collective-permute-done.7), channel_id=1, source_target_pairs={{0,8},{4,12},{8,0},{12,4},{16,24},{20,28},{24,16},{28,20},{1,9},{5... | collective-permute-start | bytes 3538952 | tf_op jit(solution)/shard_map/ppermute | solution.py:16
  962.3 27.2 %collective-permute-start.9 = (bf16[384,1536]{0,1:T(8,128)(2,1)S(1)}, bf16[384,1536]{0,1:T(8,128)(2,1)S(1)}, u32[]{:S(2)}, u32[]{:S(2)}) collective-permute-start(bf16[384,1536]{0,1:T(8,128)(2,1)S(1)} %collective-permute-done.8), channel_id=1, source_target_pairs={{0,16},{4,20},{8,24},{12,28},{16,0},{20,4},{24,8},{28,12},{1,17},{... | collective-permute-start | bytes 3538952 | tf_op jit(solution)/shard_map/ppermute | solution.py:16
  (37 other events, 298.9 us)
Sparse Core Ops, SparseCore 0:
  69.3 90.6 all-gather.1
  738.2 189.9 reduce-scatter.3
where the time goes:
time: 1000 us
  waiting for transfers between devices  534 us (53%)
  starting transfers between devices  206 us (21%)
  other arithmetic  78.3 us (8%)
  matrix products  75.6 us (8%)
  local copies, waits for them, and re-layouts  60.3 us (6%)
  loops' own time  32.7 us (3%)
  between operations  14.2 us (1%)
    ppermute x44, waiting for transfers between devices, passed_along(): return lax.ppermute(block, axis, route)  236 us
    ppermute x44, starting transfers between devices, passed_along(): return lax.ppermute(block, axis, route)  198 us
    unnamed x3, waiting for transfers between devices  190 us
    ppermute x6, waiting for transfers between devices, from_partner(): lax.ppermute(array, axis, [(i, i ^ 1 << apart) for i in range(lax.axis_si...  108 us
    dot_general x8, matrix products, forward_layer(): pre_act = jnp.dot(hidden, weight, preferred_element_type=jnp.float32)  38.5 us
    dot_general x8, matrix products, backward_layer(): lax.dot_general(grad_pre, weight, (((1,), (1,)), ((), ())), preferred_ele...  31.8 us
    dynamic_slice x44, local copies, waits for them, and re-layouts, local(): up_state, unused = lax.scan(up_forward, empty_forward(up_input), step_ids)  28.1 us
    another operation x16, other arithmetic  22.7 us
  transfers between devices with their start and end apart: 52, of which 51 were waited for; matrix products, arithmetic and copies ran while one was open for 9% of the time, Pallas kernels for 0%

commit v1 on v0

v1 whole, which is shorter than its diff:
```python
import functools

import jax
import jax.numpy as jnp
from jax import lax
from jax.experimental import pallas as pl
from jax.experimental.pallas import tpu as pltpu
from jax.sharding import PartitionSpec as P

NORM_EPS = 1e-06
MESH = pl.DeviceIdType.MESH
F32 = jnp.float32
BF16 = jnp.bfloat16


def window_kernel(
    sections,
    replicas,
    up_in,
    down_in,
    up_ct,
    down_ct,
    weight,
    out,
    grads,
    wgrad,
    vin,
    y,
    hid,
    hid_t,
    slope,
    inv,
    gin,
    gp,
    gout,
    gh,
    rs_send,
    rs_recv,
    load_sem,
    fs_sem,
    fr_sem,
    bs_sem,
    br_sem,
    oms_sem,
    omr_sem,
    gms_sem,
    gmr_sem,
    rss_sem,
    rsr_sem,
):
    p = lax.axis_index("pipe")
    z = lax.axis_index("dp")
    steps, rows, width = vin.shape
    micro = steps // 2
    last = sections - 1
    after = lax.rem(p + 1, sections)
    before = lax.rem(p + sections - 1, sections)
    mirror = last - p
    z_next = lax.rem(z + 1, replicas)
    z_prev = lax.rem(z + replicas - 1, replicas)
    tile = 512 if width % 512 == 0 else width
    tiles = width // tile
    blocks = rs_send.shape[1]
    block_w = width // blocks
    chunk_rows = width // replicas

    barrier = pltpu.get_barrier_semaphore()
    for peer in ((after, z), (before, z), (mirror, z), (p, z_next), (p, z_prev)):
        pl.semaphore_signal(barrier, inc=1, device_id=peer, device_id_type=MESH)

    def load(source, target, index):
        return pltpu.make_async_copy(source, target, load_sem.at[index])

    @pl.when(p == 0)
    def _():
        load(down_in, vin.at[pl.ds(0, micro)], 0).start()
        load(up_in, vin.at[pl.ds(micro, micro)], 1).start()

    @pl.when(p == last)
    def _():
        load(down_ct, gin.at[pl.ds(0, micro)], 2).start()
        load(up_ct, gin.at[pl.ds(micro, micro)], 3).start()

    pl.semaphore_wait(barrier, 5)

    def forward_send(i, t):
        part = pl.ds(t * tile, tile)
        return pltpu.make_async_remote_copy(
            src_ref=y.at[i, :, part],
            dst_ref=vin.at[i, :, part],
            send_sem=fs_sem.at[i, t],
            recv_sem=fr_sem.at[i, t],
            device_id=(after, z),
            device_id_type=MESH,
        )

    def backward_send(i):
        return pltpu.make_async_remote_copy(
            src_ref=gout.at[i],
            dst_ref=gin.at[i],
            send_sem=bs_sem.at[i],
            recv_sem=br_sem.at[i],
            device_id=(before, z),
            device_id_type=MESH,
        )

    def mirror_send(source, target, send_sem, recv_sem, i):
        return pltpu.make_async_remote_copy(
            src_ref=source.at[i],
            dst_ref=target.at[1, i],
            send_sem=send_sem.at[i],
            recv_sem=recv_sem.at[i],
            device_id=(mirror, z),
            device_id_type=MESH,
        )

    def keep(source, target, sem, i):
        return pltpu.make_async_copy(source.at[i], target.at[0, i - micro], sem.at[i])

    @pl.when(p == 0)
    def _():
        load(down_in, vin.at[pl.ds(0, micro)], 0).wait()
        load(up_in, vin.at[pl.ds(micro, micro)], 1).wait()

    def forward(i, carry):
        @pl.when(p > 0)
        def _():
            for t in range(tiles):
                forward_send(i, t).wait_recv()

        v = vin[i].astype(F32)
        s = lax.rsqrt(jnp.mean(v * v, axis=-1, keepdims=True) + NORM_EPS)
        hidden = (v * s).astype(BF16)
        hid[i] = hidden
        inv[i] = jnp.broadcast_to(s, (rows, 128))
        for t in range(tiles):
            cols = slice(t * tile, (t + 1) * tile)
            pre = jnp.dot(hidden, weight[0, :, cols], preferred_element_type=F32)
            sigma = 1.0 / (1.0 + jnp.exp(-pre))
            y[i, :, cols] = (vin[i, :, cols].astype(F32) + pre * sigma).astype(BF16)

            @pl.when(p < last)
            def _():
                forward_send(i, t).start()

            slope[i, :, cols] = sigma * (1.0 + pre * (1.0 - sigma))

        @pl.when(i < micro)
        def _():
            mirror_send(y, out, oms_sem, omr_sem, i).start()

        @pl.when(i >= micro)
        def _():
            keep(y, out, oms_sem, i).start()

        return carry

    lax.fori_loop(0, steps, forward, 0)

    def transpose_hidden():
        per = 128 // rows
        for j in range(steps // per):
            block = hid[j * per : (j + 1) * per].reshape(per * rows, width)
            hid_t[:, j * 128 : (j + 1) * 128] = block.T

    @pl.when(p < sections // 2)
    def _():
        transpose_hidden()

    @pl.when(p == last)
    def _():
        load(down_ct, gin.at[pl.ds(0, micro)], 2).wait()
        load(up_ct, gin.at[pl.ds(micro, micro)], 3).wait()

    def backward(i, carry):
        @pl.when(p < last)
        def _():
            backward_send(i).wait_recv()

        g = gin[i].astype(F32)
        grad_pre = (g * slope[i]).astype(BF16)
        gp[i] = grad_pre
        dots = jnp.zeros((rows, 1), F32)
        for t in range(tiles):
            cols = slice(t * tile, (t + 1) * tile)
            part = lax.dot_general(
                grad_pre,
                weight[0, cols, :],
                (((1,), (1,)), ((), ())),
                preferred_element_type=F32,
            )
            gh[:, cols] = part
            dots += jnp.sum(part * vin[i, :, cols].astype(F32), axis=-1, keepdims=True)
        s = inv[i][:, :1]
        factor = s * s * (dots * (1.0 / width))
        for t in range(tiles):
            cols = slice(t * tile, (t + 1) * tile)
            v = vin[i, :, cols].astype(F32)
            gout[i, :, cols] = (
                gin[i, :, cols].astype(F32) + s * (gh[:, cols] - v * factor)
            ).astype(BF16)

        @pl.when(p > 0)
        def _():
            backward_send(i).start()

        @pl.when(i < micro)
        def _():
            mirror_send(gout, grads, gms_sem, gmr_sem, i).start()

        @pl.when(i >= micro)
        def _():
            keep(gout, grads, gms_sem, i).start()

        return carry

    lax.fori_loop(0, steps, backward, 0)

    @pl.when(p >= sections // 2)
    def _():
        transpose_hidden()

    def piece(chunk, b):
        left = hid_t[pl.ds(pl.multiple_of(chunk * chunk_rows, chunk_rows), chunk_rows), :]
        right = gp[:, :, b * block_w : (b + 1) * block_w].reshape(steps * rows, block_w)
        return jnp.dot(left, right, preferred_element_type=F32)

    order = []
    for b in range(blocks // 2):
        order += [(b, 1), (blocks // 2 + b, -1)]

    def ring_send(s, b, way):
        return pltpu.make_async_remote_copy(
            src_ref=rs_send.at[s, b],
            dst_ref=rs_recv.at[s, b],
            send_sem=rss_sem.at[s, b],
            recv_sem=rsr_sem.at[s, b],
            device_id=(p, z_next if way > 0 else z_prev),
            device_id_type=MESH,
        )

    for b, way in order:
        chunk = lax.rem(z - way + replicas, replicas)
        rs_send[0, b] = piece(chunk, b).astype(BF16)
        ring_send(0, b, way).start()

    def ring(s, carry):
        for b, way in order:
            chunk = lax.rem(z - way * (1 + s) + replicas, replicas)
            own = piece(chunk, b)
            ring_send(s - 1, b, way).wait_recv()
            rs_send[s, b] = (own + rs_recv[s - 1, b].astype(F32)).astype(BF16)
            ring_send(s, b, way).start()
        return carry

    lax.fori_loop(1, replicas - 1, ring, 0)

    for b, way in order:
        wgrad[0, :, b * block_w : (b + 1) * block_w] = piece(z, b)
    for b, way in order:
        ring_send(replicas - 2, b, way).wait_recv()
        cols = slice(b * block_w, (b + 1) * block_w)
        wgrad[0, :, cols] = wgrad[0, :, cols] + rs_recv[replicas - 2, b].astype(F32)

    def drain(i, carry):
        @pl.when(p < last)
        def _():
            for t in range(tiles):
                forward_send(i, t).wait_send()

        @pl.when(p > 0)
        def _():
            backward_send(i).wait_send()

        @pl.when(i < micro)
        def _():
            mirror_send(y, out, oms_sem, omr_sem, i).wait()
            mirror_send(gout, grads, gms_sem, gmr_sem, i).wait()

        @pl.when(i >= micro)
        def _():
            keep(y, out, oms_sem, i).wait()
            keep(gout, grads, gms_sem, i).wait()

        return carry

    lax.fori_loop(0, steps, drain, 0)

    def ring_drain(s, carry):
        for b, way in order:
            ring_send(s, b, way).wait_send()
        return carry

    lax.fori_loop(0, replicas - 1, ring_drain, 0)


def local(up_input, down_input, up_cotangent, down_cotangent, weights):
    sections = lax.axis_size("pipe")
    replicas = lax.axis_size("dp")
    micro, rows, width = up_input.shape
    steps = 2 * micro
    chunk_rows = width // replicas
    blocks = 4
    tiles = width // 512 if width % 512 == 0 else 1
    block_w = width // blocks
    acts = (steps, rows, width)
    anywhere = pl.BlockSpec(memory_space=pl.ANY)
    vmem = pl.BlockSpec(memory_space=pltpu.VMEM)
    dma = pltpu.SemaphoreType.DMA
    flops = 6 * steps * rows * width * width
    outs, grads, wgrad = pl.pallas_call(
        functools.partial(window_kernel, sections, replicas),
        out_shape=(
            jax.ShapeDtypeStruct((2, micro, rows, width), BF16),
            jax.ShapeDtypeStruct((2, micro, rows, width), BF16),
            jax.ShapeDtypeStruct((1, chunk_rows, width), F32),
        ),
        in_specs=[anywhere] * 4 + [vmem],
        out_specs=(anywhere, anywhere, vmem),
        scratch_shapes=[
            pltpu.VMEM(acts, BF16),
            pltpu.VMEM(acts, BF16),
            pltpu.VMEM(acts, BF16),
            pltpu.VMEM((width, steps * rows), BF16),
            pltpu.VMEM(acts, F32),
            pltpu.VMEM((steps, rows, 128), F32),
            pltpu.VMEM(acts, BF16),
            pltpu.VMEM(acts, BF16),
            pltpu.VMEM(acts, BF16),
            pltpu.VMEM((rows, width), F32),
            pltpu.VMEM((replicas - 1, blocks, chunk_rows, block_w), BF16),
            pltpu.VMEM((replicas - 1, blocks, chunk_rows, block_w), BF16),
            dma((4,)),
            dma((steps, tiles)),
            dma((steps, tiles)),
            dma((steps,)),
            dma((steps,)),
            dma((steps,)),
            dma((steps,)),
            dma((steps,)),
            dma((steps,)),
            dma((replicas - 1, blocks)),
            dma((replicas - 1, blocks)),
        ],
        compiler_params=pltpu.CompilerParams(
            collective_id=0, has_side_effects=True, vmem_limit_bytes=50 * 1024 * 1024
        ),
        cost_estimate=pl.CostEstimate(
            flops=flops, bytes_accessed=20 * 1024 * 1024, transcendentals=steps * rows * width
        ),
    )(up_input, down_input, up_cotangent, down_cotangent, weights)
    return (outs[:, None], grads[:, None], wgrad)


def solution(mesh):
    return jax.shard_map(
        local,
        mesh=mesh,
        in_specs=(
            P(None, "dp", None),
            P(None, "dp", None),
            P(None, "dp", None),
            P(None, "dp", None),
            P("pipe", None, None),
        ),
        out_specs=(
            P(None, "pipe", None, "dp", None),
            P(None, "pipe", None, "dp", None),
            P("pipe", "dp", None),
        ),
        check_vma=False,
    )
```

time: 1000 us -> 225 us (0.23)
  waiting for transfers between devices: 534 us -> 0 us
  Pallas kernels: 0 us -> 213 us
  starting transfers between devices: 206 us -> 0 us
  other arithmetic: 78.3 us -> 0 us
  matrix products: 75.6 us -> 0 us
  local copies, waits for them, and re-layouts: 60.3 us -> 10.9 us
  loops' own time: 32.7 us -> 0 us
  between operations: 14.2 us -> 0.66 us
    ppermute x50 -> x0, waiting for transfers between devices: 344 us -> none  [the longest x44 236 us: passed_along(): return lax.ppermute(block, axis, route)]
    pallas_call x0 -> x1, Pallas kernels: none -> 213 us  [local(): pl.pallas_call(functools.partial(window_kernel, sections, replicas), out_...]
    ppermute x50 -> x0, starting transfers between devices: 206 us -> none  [the longest x44 198 us: passed_along(): return lax.ppermute(block, axis, route)]
    unnamed x3 -> x0, waiting for transfers between devices: 190 us -> none
    dot_general x17 -> x0, matrix products: 75.6 us -> none  [the longest x8 38.5 us: forward_layer(): pre_act = jnp.dot(hidden, weight, preferred_element_type=jnp.float32)]
    scatter x24 -> x0, other arithmetic: 43.2 us -> none  [the longest x8 20.1 us: backward_compute(): saved_dpre.at[slot_index].set(grad_pre)]
    another operation x48 -> x0, loops' own time: 32.7 us -> none  [the longest x1 7.98 us: local(): up_state, unused = lax.scan(up_forward, empty_forward(up_input), step_ids)]
    dynamic_slice x45 -> x0, local copies, waits for them, and re-layouts: 29.4 us -> none  [the longest x44 28.1 us: local(): up_state, unused = lax.scan(up_forward, empty_forward(up_input), step_ids)]
  transfers between devices with their start and end apart: 52 -> 0, of which waited for: 51 -> 0; matrix products, arithmetic and copies ran while one was open for 9% -> 0% of each run, Pallas kernels for 0% -> 0%
where the time goes in v1:
time: 225 us
  Pallas kernels  213 us (95%)
  local copies, waits for them, and re-layouts  10.9 us (5%)
    pallas_call x1, Pallas kernels, local(): pl.pallas_call(functools.partial(window_kernel, sections, replicas), out_...  213 us
    unnamed x15, local copies, waits for them, and re-layouts  10.9 us

profile of v1, /device:TPU:0, one launch (start us, length us, event | category | flops | bytes accessed | tf_op | source)
XLA Modules:
  0.0 224.8 jit_solution(7386008737291192522)
XLA Ops:
  0.6 0.0 copy-start
  0.6 1.1 copy-done
  1.8 0.0 copy-start.1
  1.8 1.1 copy-done.1
  2.9 0.0 copy-start.2
  2.9 1.1 copy-done.2
  4.0 0.0 copy-start.3
  4.0 1.1 copy-done.3
  5.2 213.2 %shard_map.76 = (bf16[2,4,64,1536]{3,2,1,0:T(8,128)(2,1)}, bf16[2,4,64,1536]{3,2,1,0:T(8,128)(2,1)}, f32[1,384,1536]{2,1,0:T(8,128)}) custom-call(bf16[4,64,1536]{2,1,0:T(8,128)(2,1)S(1)} %copy-done, bf16[4,64,1536]{2,1,0:T(8,128)(2,1)S(1)} %copy-done.1, bf16[4,64,1536]{2,1,0:T(8,128)(2,1)S(1)} %copy-done.2, bf16[4,64,1536]{2,1,0:T(8,128)(2,1)S(1)} %copy-done.3, ...), custom_call_target="tpu_custom_call" | custom-call | flops 7247757312 | bytes 20971520 | tf_op jit(solution)/shard_map/pallas_call | solution.py:311
  218.4 0.0 copy-start.5
  218.4 2.8 %copy.13 = bf16[2,1,4,64,1536]{4,3,2,1,0:T(8,128)(2,1)} copy(bf16[2,1,4,64,1536]{4,3,2,1,0:T(8,128)(2,1)} %bitcast.7) | data formatting | bytes 3145728
  221.2 0.0 copy-done.5
  221.2 0.0 copy-start.4
  221.2 1.1 copy.14
  222.3 1.1 copy-done.4
  223.4 1.4 copy.15
Async XLA Ops:
  0.6 1.1 copy-start
  1.8 1.1 copy-start.1
  2.9 1.1 copy-start.2
  4.0 1.1 copy-start.3
  218.4 2.8 %copy-start.5 = (bf16[2,4,64,1536]{3,2,1,0:T(8,128)(2,1)S(1)}, bf16[2,4,64,1536]{3,2,1,0:T(8,128)(2,1)}, u32[]{:S(2)}) copy-start(bf16[2,4,64,1536]{3,2,1,0:T(8,128)(2,1)} %get-tuple-element.7) | copy-start | bytes 4718596
  221.2 2.2 copy-start.4

commit v2 on v1

--- a/solution.py
+++ b/solution.py
@@ -8,6 +8,7 @@
 from jax.sharding import PartitionSpec as P
 
 NORM_EPS = 1e-06
+LEAD = 4
 MESH = pl.DeviceIdType.MESH
 F32 = jnp.float32
 BF16 = jnp.bfloat16
@@ -20,10 +21,12 @@
     down_in,
     up_ct,
     down_ct,
-    weight,
+    weight_hbm,
     out,
     grads,
     wgrad,
+    weight,
+    weight_t,
     vin,
     y,
     hid,
@@ -71,6 +74,8 @@
     def load(source, target, index):
         return pltpu.make_async_copy(source, target, load_sem.at[index])
 
+    load(weight_hbm.at[0], weight, 4).start()
+
     @pl.when(p == 0)
     def _():
         load(down_in, vin.at[pl.ds(0, micro)], 0).start()
@@ -80,8 +85,6 @@
     def _():
         load(down_ct, gin.at[pl.ds(0, micro)], 2).start()
         load(up_ct, gin.at[pl.ds(micro, micro)], 3).start()
-
-    pl.semaphore_wait(barrier, 5)
 
     def forward_send(i, t):
         part = pl.ds(t * tile, tile)
@@ -122,7 +125,24 @@
         load(down_in, vin.at[pl.ds(0, micro)], 0).wait()
         load(up_in, vin.at[pl.ds(micro, micro)], 1).wait()
 
-    def forward(i, carry):
+    load(weight_hbm.at[0], weight, 4).wait()
+    pl.semaphore_wait(barrier, 5)
+
+    def transpose_weight():
+        def strip(j, carry):
+            rows_of = pl.ds(pl.multiple_of(j * 128, 128), 128)
+            for k in range(width // 256):
+                cols = slice(k * 256, (k + 1) * 256)
+                weight_t[cols, rows_of] = weight[rows_of, cols].T
+            return carry
+
+        lax.fori_loop(0, width // 128, strip, 0)
+
+    @pl.when(p >= sections // 2)
+    def _():
+        transpose_weight()
+
+    def forward(i):
         @pl.when(p > 0)
         def _():
             for t in range(tiles):
@@ -135,7 +155,7 @@
         inv[i] = jnp.broadcast_to(s, (rows, 128))
         for t in range(tiles):
             cols = slice(t * tile, (t + 1) * tile)
-            pre = jnp.dot(hidden, weight[0, :, cols], preferred_element_type=F32)
+            pre = jnp.dot(hidden, weight[:, cols], preferred_element_type=F32)
             sigma = 1.0 / (1.0 + jnp.exp(-pre))
             y[i, :, cols] = (vin[i, :, cols].astype(F32) + pre * sigma).astype(BF16)
 
@@ -145,17 +165,9 @@
 
             slope[i, :, cols] = sigma * (1.0 + pre * (1.0 - sigma))
 
-        @pl.when(i < micro)
-        def _():
-            mirror_send(y, out, oms_sem, omr_sem, i).start()
-
         @pl.when(i >= micro)
         def _():
             keep(y, out, oms_sem, i).start()
-
-        return carry
-
-    lax.fori_loop(0, steps, forward, 0)
 
     def transpose_hidden():
         per = 128 // rows
@@ -163,16 +175,12 @@
             block = hid[j * per : (j + 1) * per].reshape(per * rows, width)
             hid_t[:, j * 128 : (j + 1) * 128] = block.T
 
-    @pl.when(p < sections // 2)
-    def _():
-        transpose_hidden()
-
     @pl.when(p == last)
     def _():
         load(down_ct, gin.at[pl.ds(0, micro)], 2).wait()
         load(up_ct, gin.at[pl.ds(micro, micro)], 3).wait()
 
-    def backward(i, carry):
+    def backward(i):
         @pl.when(p < last)
         def _():
             backward_send(i).wait_recv()
@@ -183,12 +191,7 @@
         dots = jnp.zeros((rows, 1), F32)
         for t in range(tiles):
             cols = slice(t * tile, (t + 1) * tile)
-            part = lax.dot_general(
-                grad_pre,
-                weight[0, cols, :],
-                (((1,), (1,)), ((), ())),
-                preferred_element_type=F32,
-            )
+            part = jnp.dot(grad_pre, weight_t[:, cols], preferred_element_type=F32)
             gh[:, cols] = part
             dots += jnp.sum(part * vin[i, :, cols].astype(F32), axis=-1, keepdims=True)
         s = inv[i][:, :1]
@@ -204,21 +207,33 @@
         def _():
             backward_send(i).start()
 
-        @pl.when(i < micro)
-        def _():
-            mirror_send(gout, grads, gms_sem, gmr_sem, i).start()
-
         @pl.when(i >= micro)
         def _():
             keep(gout, grads, gms_sem, i).start()
 
-        return carry
-
-    lax.fori_loop(0, steps, backward, 0)
-
-    @pl.when(p >= sections // 2)
-    def _():
-        transpose_hidden()
+    lead = jnp.minimum(steps, LEAD * (last - p))
+
+    def turn(t, carry):
+        @pl.when(t < steps)
+        def _():
+            forward(t)
+
+        @pl.when(t == steps - 1)
+        def _():
+            transpose_hidden()
+
+            @pl.when(p < sections // 2)
+            def _():
+                transpose_weight()
+
+
+        @pl.when(t >= lead)
+        def _():
+            backward(t - lead)
+
+        return carry
+
+    lax.fori_loop(0, steps + lead, turn, 0)
 
     def piece(chunk, b):
         left = hid_t[pl.ds(pl.multiple_of(chunk * chunk_rows, chunk_rows), chunk_rows), :]
@@ -243,6 +258,13 @@
         chunk = lax.rem(z - way + replicas, replicas)
         rs_send[0, b] = piece(chunk, b).astype(BF16)
         ring_send(0, b, way).start()
+
+    def to_mirror(i, carry):
+        mirror_send(y, out, oms_sem, omr_sem, i).start()
+        mirror_send(gout, grads, gms_sem, gmr_sem, i).start()
+        return carry
+
+    lax.fori_loop(0, micro, to_mirror, 0)
 
     def ring(s, carry):
         for b, way in order:
@@ -304,7 +326,7 @@
     tiles = width // 512 if width % 512 == 0 else 1
     block_w = width // blocks
     acts = (steps, rows, width)
-    anywhere = pl.BlockSpec(memory_space=pl.ANY)
+    anywhere = pl.BlockSpec(memory_space=pltpu.HBM)
     vmem = pl.BlockSpec(memory_space=pltpu.VMEM)
     dma = pltpu.SemaphoreType.DMA
     flops = 6 * steps * rows * width * width
@@ -315,9 +337,11 @@
             jax.ShapeDtypeStruct((2, micro, rows, width), BF16),
             jax.ShapeDtypeStruct((1, chunk_rows, width), F32),
         ),
-        in_specs=[anywhere] * 4 + [vmem],
+        in_specs=[anywhere] * 5,
         out_specs=(anywhere, anywhere, vmem),
         scratch_shapes=[
+            pltpu.VMEM((width, width), BF16),
+            pltpu.VMEM((width, width), BF16),
             pltpu.VMEM(acts, BF16),
             pltpu.VMEM(acts, BF16),
             pltpu.VMEM(acts, BF16),
@@ -330,7 +354,7 @@
             pltpu.VMEM((rows, width), F32),
             pltpu.VMEM((replicas - 1, blocks, chunk_rows, block_w), BF16),
             pltpu.VMEM((replicas - 1, blocks, chunk_rows, block_w), BF16),
-            dma((4,)),
+            dma((5,)),
             dma((steps, tiles)),
             dma((steps, tiles)),
             dma((steps,)),

time: 225 us -> 178 us (0.79)
  Pallas kernels: 213 us -> 166 us
    pallas_call x1, Pallas kernels: 213 us -> 166 us  [local(): pl.pallas_call(functools.partial(window_kernel, sections, replicas), out_...]
where the time goes in v2:
time: 178 us
  Pallas kernels  166 us (93%)
  local copies, waits for them, and re-layouts  10.9 us (6%)
    pallas_call x1, Pallas kernels, local(): pl.pallas_call(functools.partial(window_kernel, sections, replicas), out_...  166 us
    unnamed x15, local copies, waits for them, and re-layouts  10.9 us

profile of v2, /device:TPU:0, one launch (start us, length us, event | category | flops | bytes accessed | tf_op | source)
XLA Modules:
  0.0 178.0 jit_solution(13007502077502389895)
XLA Ops:
  0.6 0.0 copy-start
  0.6 1.1 copy-done
  1.8 0.0 copy-start.1
  1.8 1.1 copy-done.1
  2.9 0.0 copy-start.2
  2.9 1.1 copy-done.2
  4.0 0.0 copy-start.3
  4.0 1.1 copy-done.3
  5.2 166.4 %shard_map.76 = (bf16[2,4,64,1536]{3,2,1,0:T(8,128)(2,1)}, bf16[2,4,64,1536]{3,2,1,0:T(8,128)(2,1)}, f32[1,384,1536]{2,1,0:T(8,128)}) custom-call(bf16[4,64,1536]{2,1,0:T(8,128)(2,1)S(1)} %copy-done, bf16[4,64,1536]{2,1,0:T(8,128)(2,1)S(1)} %copy-done.1, bf16[4,64,1536]{2,1,0:T(8,128)(2,1)S(1)} %copy-done.2, bf16[4,64,1536]{2,1,0:T(8,128)(2,1)S(1)} %copy-done.3, ...), custom_call_target="tpu_custom_call" | custom-call | flops 7247757312 | bytes 20971520 | tf_op jit(solution)/shard_map/pallas_call | solution.py:333
  171.6 0.0 copy-start.5
  171.6 2.8 %copy.13 = bf16[2,1,4,64,1536]{4,3,2,1,0:T(8,128)(2,1)} copy(bf16[2,1,4,64,1536]{4,3,2,1,0:T(8,128)(2,1)} %bitcast.7) | data formatting | bytes 3145728
  174.4 0.0 copy-done.5
  174.4 0.0 copy-start.4
  174.4 1.1 copy.14
  175.5 1.1 copy-done.4
  176.6 1.4 copy.15
Async XLA Ops:
  0.6 1.1 copy-start
  1.8 1.1 copy-start.1
  2.9 1.1 copy-start.2
  4.0 1.1 copy-start.3
  171.6 2.8 %copy-start.5 = (bf16[2,4,64,1536]{3,2,1,0:T(8,128)(2,1)S(1)}, bf16[2,4,64,1536]{3,2,1,0:T(8,128)(2,1)}, u32[]{:S(2)}) copy-start(bf16[2,4,64,1536]{3,2,1,0:T(8,128)(2,1)} %get-tuple-element.7) | copy-start | bytes 4718596
  174.4 2.2 %copy-start.4 = (f32[1,384,1536]{2,1,0:T(8,128)S(1)}, f32[1,384,1536]{2,1,0:T(8,128)}, u32[]{:S(2)}) copy-start(f32[1,384,1536]{2,1,0:T(8,128)} %get-tuple-element.17) | copy-start | bytes 7077892

commit v3 on v2

--- a/solution.py
+++ b/solution.py
@@ -39,6 +39,10 @@
     gh,
     rs_send,
     rs_recv,
+    tail_send,
+    tail_recv,
+    pair_hid,
+    pair_gp,
     load_sem,
     fs_sem,
     fr_sem,
@@ -50,6 +54,14 @@
     gmr_sem,
     rss_sem,
     rsr_sem,
+    ts_sem,
+    tr_sem,
+    phs_sem,
+    phr_sem,
+    pgs_sem,
+    pgr_sem,
+    pbs_sem,
+    pbr_sem,
 ):
     p = lax.axis_index("pipe")
     z = lax.axis_index("dp")
@@ -117,6 +129,66 @@
             device_id_type=MESH,
         )
 
+    line = replicas == 4
+    eager = steps // 2
+    is_end = jnp.logical_or(z == 0, z == replicas - 1)
+    pair = z + 1 - 2 * lax.rem(z, 2)
+    middle = jnp.where(z == 1, 2, 1)
+    far = jnp.where(z == 1, 3, 0)
+    kept = width - chunk_rows
+
+    def pair_hid_send():
+        part = pl.ds(pl.multiple_of(jnp.where(z == 0, chunk_rows, 0), chunk_rows), kept)
+        return pltpu.make_async_remote_copy(
+            src_ref=hid_t.at[part],
+            dst_ref=pair_hid.at[part],
+            send_sem=phs_sem.at[0],
+            recv_sem=phr_sem.at[0],
+            device_id=(p, pair),
+            device_id_type=MESH,
+        )
+
+    def pair_gp_send(i):
+        return pltpu.make_async_remote_copy(
+            src_ref=gp.at[i],
+            dst_ref=pair_gp.at[i],
+            send_sem=pgs_sem.at[i],
+            recv_sem=pgr_sem.at[i],
+            device_id=(p, pair),
+            device_id_type=MESH,
+        )
+
+    def pair_block_send(j):
+        part = (pl.ds(eager, steps - eager), slice(None), pl.ds(j * block_w, block_w))
+        return pltpu.make_async_remote_copy(
+            src_ref=gp.at[part],
+            dst_ref=pair_gp.at[part],
+            send_sem=pbs_sem.at[j],
+            recv_sem=pbr_sem.at[j],
+            device_id=(p, pair),
+            device_id_type=MESH,
+        )
+
+    def middle_copy(k, j):
+        return pltpu.make_async_remote_copy(
+            src_ref=rs_send.at[k, j],
+            dst_ref=rs_recv.at[k, j],
+            send_sem=rss_sem.at[k, j],
+            recv_sem=rsr_sem.at[k, j],
+            device_id=(p, middle),
+            device_id_type=MESH,
+        )
+
+    def tail_copy(j):
+        return pltpu.make_async_remote_copy(
+            src_ref=tail_send.at[j],
+            dst_ref=tail_recv.at[j],
+            send_sem=ts_sem.at[j],
+            recv_sem=tr_sem.at[j],
+            device_id=(p, pair),
+            device_id_type=MESH,
+        )
+
     def keep(source, target, sem, i):
         return pltpu.make_async_copy(source.at[i], target.at[0, i - micro], sem.at[i])
 
@@ -188,6 +260,12 @@
         g = gin[i].astype(F32)
         grad_pre = (g * slope[i]).astype(BF16)
         gp[i] = grad_pre
+        if line:
+
+            @pl.when(jnp.logical_and(is_end, i < eager))
+            def _():
+                pair_gp_send(i).start()
+
         dots = jnp.zeros((rows, 1), F32)
         for t in range(tiles):
             cols = slice(t * tile, (t + 1) * tile)
@@ -221,6 +299,11 @@
         @pl.when(t == steps - 1)
         def _():
             transpose_hidden()
+            if line:
+
+                @pl.when(is_end)
+                def _():
+                    pair_hid_send().start()
 
             @pl.when(p < sections // 2)
             def _():
@@ -235,54 +318,93 @@
 
     lax.fori_loop(0, steps + lead, turn, 0)
 
-    def piece(chunk, b):
-        left = hid_t[pl.ds(pl.multiple_of(chunk * chunk_rows, chunk_rows), chunk_rows), :]
-        right = gp[:, :, b * block_w : (b + 1) * block_w].reshape(steps * rows, block_w)
-        return jnp.dot(left, right, preferred_element_type=F32)
-
-    order = []
-    for b in range(blocks // 2):
-        order += [(b, 1), (blocks // 2 + b, -1)]
-
-    def ring_send(s, b, way):
-        return pltpu.make_async_remote_copy(
-            src_ref=rs_send.at[s, b],
-            dst_ref=rs_recv.at[s, b],
-            send_sem=rss_sem.at[s, b],
-            recv_sem=rsr_sem.at[s, b],
-            device_id=(p, z_next if way > 0 else z_prev),
-            device_id_type=MESH,
-        )
-
-    for b, way in order:
-        chunk = lax.rem(z - way + replicas, replicas)
-        rs_send[0, b] = piece(chunk, b).astype(BF16)
-        ring_send(0, b, way).start()
+    def piece(left, right, chunk, j):
+        at = pl.multiple_of(chunk * chunk_rows, chunk_rows)
+        return jnp.dot(
+            left[pl.ds(at, chunk_rows), :],
+            right[:, :, j * block_w : (j + 1) * block_w].reshape(steps * rows, block_w),
+            preferred_element_type=F32,
+        )
 
     def to_mirror(i, carry):
         mirror_send(y, out, oms_sem, omr_sem, i).start()
         mirror_send(gout, grads, gms_sem, gmr_sem, i).start()
         return carry
 
-    lax.fori_loop(0, micro, to_mirror, 0)
-
-    def ring(s, carry):
-        for b, way in order:
-            chunk = lax.rem(z - way * (1 + s) + replicas, replicas)
-            own = piece(chunk, b)
-            ring_send(s - 1, b, way).wait_recv()
-            rs_send[s, b] = (own + rs_recv[s - 1, b].astype(F32)).astype(BF16)
-            ring_send(s, b, way).start()
-        return carry
-
-    lax.fori_loop(1, replicas - 1, ring, 0)
-
-    for b, way in order:
-        wgrad[0, :, b * block_w : (b + 1) * block_w] = piece(z, b)
-    for b, way in order:
-        ring_send(replicas - 2, b, way).wait_recv()
-        cols = slice(b * block_w, (b + 1) * block_w)
-        wgrad[0, :, cols] = wgrad[0, :, cols] + rs_recv[replicas - 2, b].astype(F32)
+    if line:
+
+        @pl.when(is_end)
+        def _():
+            for j in range(blocks):
+                pair_block_send(j).start()
+            lax.fori_loop(0, micro, to_mirror, 0)
+            for j in range(blocks):
+                cols = slice(j * block_w, (j + 1) * block_w)
+                own = piece(hid_t, gp, z, j)
+                tail_copy(j).wait_recv()
+                wgrad[0, :, cols] = own + tail_recv[j].astype(F32)
+
+        @pl.when(jnp.logical_not(is_end))
+        def _():
+            pair_hid_send().wait_recv()
+            for i in range(eager):
+                pair_gp_send(i).wait_recv()
+            for j in range(blocks):
+                pair_block_send(j).wait_recv()
+                for k, chunk in enumerate((far, middle)):
+                    total = piece(hid_t, gp, chunk, j) + piece(pair_hid, pair_gp, chunk, j)
+                    rs_send[k, j] = total.astype(BF16)
+                    middle_copy(k, j).start()
+            lax.fori_loop(0, micro, to_mirror, 0)
+            for j in range(blocks):
+                cols = slice(j * block_w, (j + 1) * block_w)
+                own = piece(hid_t, gp, pair, j)
+                middle_copy(0, j).wait_recv()
+                tail_send[j] = (own + rs_recv[0, j].astype(F32)).astype(BF16)
+                tail_copy(j).start()
+                own = piece(hid_t, gp, z, j) + piece(pair_hid, pair_gp, z, j)
+                middle_copy(1, j).wait_recv()
+                wgrad[0, :, cols] = own + rs_recv[1, j].astype(F32)
+
+    else:
+
+        def ring_send(s, j, way):
+            return pltpu.make_async_remote_copy(
+                src_ref=rs_send.at[s, j],
+                dst_ref=rs_recv.at[s, j],
+                send_sem=rss_sem.at[s, j],
+                recv_sem=rsr_sem.at[s, j],
+                device_id=(p, z_next if way > 0 else z_prev),
+                device_id_type=MESH,
+            )
+
+        order = []
+        for j in range(blocks // 2):
+            order += [(j, 1), (blocks // 2 + j, -1)]
+
+        for j, way in order:
+            chunk = lax.rem(z - way + replicas, replicas)
+            rs_send[0, j] = piece(hid_t, gp, chunk, j).astype(BF16)
+            ring_send(0, j, way).start()
+
+        lax.fori_loop(0, micro, to_mirror, 0)
+
+        def ring(s, carry):
+            for j, way in order:
+                chunk = lax.rem(z - way * (1 + s) + replicas, replicas)
+                own = piece(hid_t, gp, chunk, j)
+                ring_send(s - 1, j, way).wait_recv()
+                rs_send[s, j] = (own + rs_recv[s - 1, j].astype(F32)).astype(BF16)
+                ring_send(s, j, way).start()
+            return carry
+
+        lax.fori_loop(1, replicas - 1, ring, 0)
+
+        for j, way in order:
+            cols = slice(j * block_w, (j + 1) * block_w)
+            own = piece(hid_t, gp, z, j)
+            ring_send(replicas - 2, j, way).wait_recv()
+            wgrad[0, :, cols] = own + rs_recv[replicas - 2, j].astype(F32)
 
     def drain(i, carry):
         @pl.when(p < last)
@@ -308,12 +430,31 @@
 
     lax.fori_loop(0, steps, drain, 0)
 
-    def ring_drain(s, carry):
-        for b, way in order:
-            ring_send(s, b, way).wait_send()
-        return carry
-
-    lax.fori_loop(0, replicas - 1, ring_drain, 0)
+    if line:
+
+        @pl.when(is_end)
+        def _():
+            pair_hid_send().wait_send()
+            for i in range(eager):
+                pair_gp_send(i).wait_send()
+            for j in range(blocks):
+                pair_block_send(j).wait_send()
+
+        @pl.when(jnp.logical_not(is_end))
+        def _():
+            for j in range(blocks):
+                middle_copy(0, j).wait_send()
+                middle_copy(1, j).wait_send()
+                tail_copy(j).wait_send()
+
+    else:
+
+        def ring_drain(s, carry):
+            for j, way in order:
+                ring_send(s, j, way).wait_send()
+            return carry
+
+        lax.fori_loop(0, replicas - 1, ring_drain, 0)
 
 
 def local(up_input, down_input, up_cotangent, down_cotangent, weights):
@@ -322,7 +463,9 @@
     micro, rows, width = up_input.shape
     steps = 2 * micro
     chunk_rows = width // replicas
-    blocks = 4
+    line = replicas == 4
+    blocks = 6 if line and width % 768 == 0 else 4
+    hops = 2 if line else replicas - 1
     tiles = width // 512 if width % 512 == 0 else 1
     block_w = width // blocks
     acts = (steps, rows, width)
@@ -352,8 +495,12 @@
             pltpu.VMEM(acts, BF16),
             pltpu.VMEM(acts, BF16),
             pltpu.VMEM((rows, width), F32),
-            pltpu.VMEM((replicas - 1, blocks, chunk_rows, block_w), BF16),
-            pltpu.VMEM((replicas - 1, blocks, chunk_rows, block_w), BF16),
+            pltpu.VMEM((hops, blocks, chunk_rows, block_w), BF16),
+            pltpu.VMEM((hops, blocks, chunk_rows, block_w), BF16),
+            pltpu.VMEM((blocks, chunk_rows, block_w), BF16),
+            pltpu.VMEM((blocks, chunk_rows, block_w), BF16),
+            pltpu.VMEM((width, steps * rows), BF16),
+            pltpu.VMEM(acts, BF16),
             dma((5,)),
             dma((steps, tiles)),
             dma((steps, tiles)),
@@ -363,8 +510,16 @@
             dma((steps,)),
             dma((steps,)),
             dma((steps,)),
-            dma((replicas - 1, blocks)),
-            dma((replicas - 1, blocks)),
+            dma((hops, blocks)),
+            dma((hops, blocks)),
+            dma((blocks,)),
+            dma((blocks,)),
+            dma((1,)),
+            dma((1,)),
+            dma((steps,)),
+            dma((steps,)),
+            dma((blocks,)),
+            dma((blocks,)),
         ],
         compiler_params=pltpu.CompilerParams(
             collective_id=0, has_side_effects=True, vmem_limit_bytes=50 * 1024 * 1024

time: 178 us -> 162 us (0.910)
  Pallas kernels: 166 us -> 150 us
    pallas_call x1, Pallas kernels: 166 us -> 150 us  [local(): pl.pallas_call(functools.partial(window_kernel, sections, replicas), out_...]
where the time goes in v3:
time: 162 us
  Pallas kernels  150 us (93%)
  local copies, waits for them, and re-layouts  10.9 us (7%)
    pallas_call x1, Pallas kernels, local(): pl.pallas_call(functools.partial(window_kernel, sections, replicas), out_...  150 us
    unnamed x15, local copies, waits for them, and re-layouts  10.9 us

profile of v3, /device:TPU:0, one launch (start us, length us, event | category | flops | bytes accessed | tf_op | source)
XLA Modules:
  0.0 162.0 jit_solution(9555935967889496829)
XLA Ops:
  0.6 0.0 copy-start
  0.6 1.1 copy-done
  1.8 0.0 copy-start.1
  1.8 1.1 copy-done.1
  2.9 0.0 copy-start.2
  2.9 1.1 copy-done.2
  4.0 0.0 copy-start.3
  4.0 1.1 copy-done.3
  5.2 150.4 %shard_map.76 = (bf16[2,4,64,1536]{3,2,1,0:T(8,128)(2,1)}, bf16[2,4,64,1536]{3,2,1,0:T(8,128)(2,1)}, f32[1,384,1536]{2,1,0:T(8,128)}) custom-call(bf16[4,64,1536]{2,1,0:T(8,128)(2,1)S(1)} %copy-done, bf16[4,64,1536]{2,1,0:T(8,128)(2,1)S(1)} %copy-done.1, bf16[4,64,1536]{2,1,0:T(8,128)(2,1)S(1)} %copy-done.2, bf16[4,64,1536]{2,1,0:T(8,128)(2,1)S(1)} %copy-done.3, ...), custom_call_target="tpu_custom_call" | custom-call | flops 7247757312 | bytes 20971520 | tf_op jit(solution)/shard_map/pallas_call | solution.py:476
  155.6 0.0 copy-start.5
  155.6 2.8 %copy.13 = bf16[2,1,4,64,1536]{4,3,2,1,0:T(8,128)(2,1)} copy(bf16[2,1,4,64,1536]{4,3,2,1,0:T(8,128)(2,1)} %bitcast.7) | data formatting | bytes 3145728
  158.3 0.0 copy-done.5
  158.4 0.0 copy-start.4
  158.4 1.1 copy.14
  159.5 1.1 copy-done.4
  160.6 1.4 copy.15
Async XLA Ops:
  0.6 1.1 copy-start
  1.8 1.1 copy-start.1
  2.9 1.1 copy-start.2
  4.0 1.1 copy-start.3
  155.6 2.8 %copy-start.5 = (bf16[2,4,64,1536]{3,2,1,0:T(8,128)(2,1)S(1)}, bf16[2,4,64,1536]{3,2,1,0:T(8,128)(2,1)}, u32[]{:S(2)}) copy-start(bf16[2,4,64,1536]{3,2,1,0:T(8,128)(2,1)} %get-tuple-element.7) | copy-start | bytes 4718596
  158.4 2.2 %copy-start.4 = (f32[1,384,1536]{2,1,0:T(8,128)S(1)}, f32[1,384,1536]{2,1,0:T(8,128)}, u32[]{:S(2)}) copy-start(f32[1,384,1536]{2,1,0:T(8,128)} %get-tuple-element.17) | copy-start | bytes 7077892

commit v4 on v3

--- a/solution.py
+++ b/solution.py
@@ -266,6 +266,11 @@
             def _():
                 pair_gp_send(i).start()
 
+            @pl.when(jnp.logical_and(is_end, i == steps - 1))
+            def _():
+                for j in range(blocks):
+                    pair_block_send(j).start()
+
         dots = jnp.zeros((rows, 1), F32)
         for t in range(tiles):
             cols = slice(t * tile, (t + 1) * tile)
@@ -335,8 +340,6 @@
 
         @pl.when(is_end)
         def _():
-            for j in range(blocks):
-                pair_block_send(j).start()
             lax.fori_loop(0, micro, to_mirror, 0)
             for j in range(blocks):
                 cols = slice(j * block_w, (j + 1) * block_w)
@@ -522,7 +525,7 @@
             dma((blocks,)),
         ],
         compiler_params=pltpu.CompilerParams(
-            collective_id=0, has_side_effects=True, vmem_limit_bytes=50 * 1024 * 1024
+            collective_id=0, has_side_effects=True, vmem_limit_bytes=63 * 1024 * 1024
         ),
         cost_estimate=pl.CostEstimate(
             flops=flops, bytes_accessed=20 * 1024 * 1024, transcendentals=steps * rows * width

time: 162 us -> 157 us (0.969)
  local copies, waits for them, and re-layouts: 10.9 us -> 6.41 us
    unnamed x15 -> x7, local copies, waits for them, and re-layouts: 10.9 us -> 6.41 us
where the time goes in v4:
time: 157 us
  Pallas kernels  150 us (96%)
  local copies, waits for them, and re-layouts  6.41 us (4%)
    pallas_call x1, Pallas kernels, local(): pl.pallas_call(functools.partial(window_kernel, sections, replicas), out_...  150 us
    unnamed x7, local copies, waits for them, and re-layouts  6.41 us

profile of v4, /device:TPU:0, one launch (start us, length us, event | category | flops | bytes accessed | tf_op | source)
XLA Modules:
  0.0 156.9 jit_solution(13689385930853900321)
XLA Ops:
  0.6 149.9 %shard_map.76 = (bf16[2,4,64,1536]{3,2,1,0:T(8,128)(2,1)}, bf16[2,4,64,1536]{3,2,1,0:T(8,128)(2,1)}, f32[1,384,1536]{2,1,0:T(8,128)}) custom-call(bf16[4,64,1536]{2,1,0:T(8,128)(2,1)} %up_in.1, bf16[4,64,1536]{2,1,0:T(8,128)(2,1)} %down_in.1, bf16[4,64,1536]{2,1,0:T(8,128)(2,1)} %up_ct.1, bf16[4,64,1536]{2,1,0:T(8,128)(2,1)} %down_ct.1, ...), custom_call_target="tpu_custom_call" | custom-call | flops 7247757312 | bytes 20971520 | tf_op jit(solution)/shard_map/pallas_call | solution.py:479
  150.5 0.0 copy-start.1
  150.5 2.8 %copy.13 = bf16[2,1,4,64,1536]{4,3,2,1,0:T(8,128)(2,1)} copy(bf16[2,1,4,64,1536]{4,3,2,1,0:T(8,128)(2,1)} %bitcast.7) | data formatting | bytes 3145728
  153.3 0.0 copy-done.1
  153.3 0.0 copy-start
  153.3 1.1 copy.14
  154.4 1.1 copy-done
  155.5 1.4 copy.15
Async XLA Ops:
  150.5 2.8 %copy-start.1 = (bf16[2,4,64,1536]{3,2,1,0:T(8,128)(2,1)S(1)}, bf16[2,4,64,1536]{3,2,1,0:T(8,128)(2,1)}, u32[]{:S(2)}) copy-start(bf16[2,4,64,1536]{3,2,1,0:T(8,128)(2,1)} %get-tuple-element.7) | copy-start | bytes 4718596
  153.3 2.2 %copy-start = (f32[1,384,1536]{2,1,0:T(8,128)S(1)}, f32[1,384,1536]{2,1,0:T(8,128)}, u32[]{:S(2)}) copy-start(f32[1,384,1536]{2,1,0:T(8,128)} %get-tuple-element.17) | copy-start | bytes 7077892

commit v5 on v4

--- a/solution.py
+++ b/solution.py
@@ -130,7 +130,7 @@
         )
 
     line = replicas == 4
-    eager = steps // 2
+    eager = steps - 2
     is_end = jnp.logical_or(z == 0, z == replicas - 1)
     pair = z + 1 - 2 * lax.rem(z, 2)
     middle = jnp.where(z == 1, 2, 1)
@@ -198,8 +198,6 @@
         load(up_in, vin.at[pl.ds(micro, micro)], 1).wait()
 
     load(weight_hbm.at[0], weight, 4).wait()
-    pl.semaphore_wait(barrier, 5)
-
     def transpose_weight():
         def strip(j, carry):
             rows_of = pl.ds(pl.multiple_of(j * 128, 128), 128)
@@ -213,6 +211,8 @@
     @pl.when(p >= sections // 2)
     def _():
         transpose_weight()
+
+    pl.semaphore_wait(barrier, 5)
 
     def forward(i):
         @pl.when(p > 0)

time: 157 us -> 156 us (level)
  no operation moved by 1% of the time
where the time goes in v5:
time: 156 us
  Pallas kernels  149 us (96%)
  local copies, waits for them, and re-layouts  6.41 us (4%)
    pallas_call x1, Pallas kernels, local(): pl.pallas_call(functools.partial(window_kernel, sections, replicas), out_...  149 us
    unnamed x7, local copies, waits for them, and re-layouts  6.41 us

profile of v5, /device:TPU:0, one launch (start us, length us, event | category | flops | bytes accessed | tf_op | source)
XLA Modules:
  0.0 156.2 jit_solution(880709200514742861)
XLA Ops:
  0.6 149.2 %shard_map.76 = (bf16[2,4,64,1536]{3,2,1,0:T(8,128)(2,1)}, bf16[2,4,64,1536]{3,2,1,0:T(8,128)(2,1)}, f32[1,384,1536]{2,1,0:T(8,128)}) custom-call(bf16[4,64,1536]{2,1,0:T(8,128)(2,1)} %up_in.1, bf16[4,64,1536]{2,1,0:T(8,128)(2,1)} %down_in.1, bf16[4,64,1536]{2,1,0:T(8,128)(2,1)} %up_ct.1, bf16[4,64,1536]{2,1,0:T(8,128)(2,1)} %down_ct.1, ...), custom_call_target="tpu_custom_call" | custom-call | flops 7247757312 | bytes 20971520 | tf_op jit(solution)/shard_map/pallas_call | solution.py:479
  149.8 0.0 copy-start.1
  149.8 2.8 %copy.13 = bf16[2,1,4,64,1536]{4,3,2,1,0:T(8,128)(2,1)} copy(bf16[2,1,4,64,1536]{4,3,2,1,0:T(8,128)(2,1)} %bitcast.7) | data formatting | bytes 3145728
  152.6 0.0 copy-done.1
  152.6 0.0 copy-start
  152.6 1.1 copy.14
  153.7 1.1 copy-done
  154.8 1.4 copy.15
Async XLA Ops:
  149.8 2.8 %copy-start.1 = (bf16[2,4,64,1536]{3,2,1,0:T(8,128)(2,1)S(1)}, bf16[2,4,64,1536]{3,2,1,0:T(8,128)(2,1)}, u32[]{:S(2)}) copy-start(bf16[2,4,64,1536]{3,2,1,0:T(8,128)(2,1)} %get-tuple-element.7) | copy-start | bytes 4718596
  152.6 2.2 %copy-start = (f32[1,384,1536]{2,1,0:T(8,128)S(1)}, f32[1,384,1536]{2,1,0:T(8,128)}, u32[]{:S(2)}) copy-start(f32[1,384,1536]{2,1,0:T(8,128)} %get-tuple-element.17) | copy-start | bytes 7077892
